TPU v7x, 256 devices: a whole 4x4x8 slice. The times are simulated.
256 devices in a mesh: dp: 64 (over y, z, x_lo), tensor: 4 (over x_hi, core).
Axes of the slice: x: 4 (x_hi: 2, x_lo: 2; x = x_hi * 2 + x_lo), y: 4, z: 8, core: 2. Of those that a mesh axis runs over, the one named last changes fastest.
Arguments:
- images: bfloat16 [180224, 1152], P(('dp', 'tensor')), may hold values from -6 to 6
- texts: bfloat16 [180224, 1152], P(('dp', 'tensor')), may hold values from -6 to 6
- logit_scale: float32 [1], replicated, may hold values from 1 to 2
- logit_bias: float32 [1], replicated, may hold values from -2 to 0
Outputs:
- image_grad: float32 [180224, 1152], P(('dp', 'tensor'))
- text_grad: float32 [180224, 1152], P(('dp', 'tensor'))
All inputs are finite; a program needn't handle non-finite values.
Results may differ from a plain program's by a relative error of at most 0.0019.
Values may be sent and summed in bfloat16 or wider, within the bound.
A program may use at most 64 MiB of HBM per device.

v0:
```python
import math

import jax
import jax.numpy as jnp
from jax import lax
from jax.sharding import PartitionSpec as P

D = 1152
STEPS = 4


def from_behind(value, axis, steps):
    count = lax.axis_size(axis)
    pairs = [(source, (source + steps) % count) for source in range(count)]
    return lax.ppermute(value, axis, pairs)


def body(images, texts, logit_scale, logit_bias):
    rows = images.shape[0]
    factor = logit_scale[0] / math.sqrt(D)
    bias_value = logit_bias[0]
    text_block = texts
    image_total = jnp.zeros(images.shape, jnp.float32)
    text_sum = jnp.zeros(texts.shape, jnp.float32)
    for step in range(STEPS):
        if step > 0:
            text_block = from_behind(text_block, ("dp", "tensor"), 1)
        logits = lax.dot_general(
            images, text_block, (((1,), (1,)), ((), ())), preferred_element_type=jnp.float32
        )
        weights = jax.nn.sigmoid(factor * logits + bias_value)
        if step == 0:
            weights = weights - jnp.eye(rows, dtype=jnp.float32)
        weights = weights.astype(jnp.bfloat16)
        image_total = image_total + factor * jnp.dot(
            weights, text_block, preferred_element_type=jnp.float32
        )
        term = factor * lax.dot_general(
            weights, images, (((0,), (0,)), ((), ())), preferred_element_type=jnp.float32
        )
        text_sum = text_sum + term
        if step + 1 < STEPS:
            text_sum = from_behind(text_sum, ("dp", "tensor"), 1)
    text_total = from_behind(text_sum, ("dp", "tensor"), 1 - STEPS)
    return (image_total, text_total)


def solution(mesh):
    in_specs = (P(("dp", "tensor"), None), P(("dp", "tensor"), None), P(), P())
    out_specs = (P(("dp", "tensor"), None), P(("dp", "tensor"), None))
    return jax.shard_map(body, mesh=mesh, in_specs=in_specs, out_specs=out_specs, check_vma=False)
```

profile of v0, /device:TPU:1, one launch (start us, length us, event | category | flops | bytes accessed | tf_op | source)
XLA Modules:
  0.0 267.0 jit_solution(15400184176936321465)
XLA Ops:
  0.6 0.0 copy-start
  2.1 0.0 copy-done
  2.1 3.2 %subtract_convert_fusion = bf16[704,704]{1,0:T(8,128)(2,1)S(1)} fusion(bf16[704,1152]{1,0:T(8,128)(2,1)S(1)} %copy-done, bf16[704,1152]{1,0:T(8,128)(2,1)} %param.5, f32[]{:T(128)} %bitcast.26, f32[]{:T(128)} %bitcast), kind=kOutput, calls=%fused_computation.12 | convolution fusion | flops 1146359808 | bytes 4235272 | tf_op jit(solution)/shard_map/dot_general | solution.py:28
  5.3 0.0 copy-start.1
  5.3 1.6 convolution_multiply_fusion.3
  6.9 4.2 %collective-permute-start.3 = (f32[704,1152]{1,0:T(8,128)S(1)}, f32[704,1152]{1,0:T(8,128)S(1)}, u32[]{:S(2)}, u32[]{:S(2)}) collective-permute-start(f32[704,1152]{1,0:T(8,128)S(1)} %convolution_multiply_fusion.3), channel_id=1, source_target_pairs={{0,1},{1,2},{2,3},{3,4},{4,5},{5,6},{6,7},{7,8},{8,9},{9,10},{10,1... | collective-permute-start | bytes 9732104 | tf_op jit(solution)/shard_map/ppermute | solution.py:15
  11.2 0.0 copy-done.1
  11.2 0.1 collective-permute-start
  11.3 52.5 %collective-permute-done = bf16[704,1152]{1,0:T(8,128)(2,1)S(1)} collective-permute-done((bf16[704,1152]{1,0:T(8,128)(2,1)S(1)}, bf16[704,1152]{1,0:T(8,128)(2,1)S(1)}, u32[]{:S(2)}, u32[]{:S(2)}) %collective-permute-start) | collective-permute-done | bytes 1622048 | tf_op jit(solution)/shard_map/ppermute | solution.py:15
  63.8 1.8 divide_convert_fusion.2
  65.6 0.0 collective-permute-done.3
  65.6 1.6 fusion
  67.3 4.1 %collective-permute-start.4 = (f32[704,1152]{1,0:T(8,128)S(1)}, f32[704,1152]{1,0:T(8,128)S(1)}, u32[]{:S(2)}, u32[]{:S(2)}) collective-permute-start(f32[704,1152]{1,0:T(8,128)S(1)} %fusion), channel_id=1, source_target_pairs={{0,1},{1,2},{2,3},{3,4},{4,5},{5,6},{6,7},{7,8},{8,9},{9,10},{10,1... | collective-permute-start | bytes 9732104 | tf_op jit(solution)/shard_map/ppermute | solution.py:15
  71.3 0.1 collective-permute-start.1
  71.4 52.6 %collective-permute-done.1 = bf16[704,1152]{1,0:T(8,128)(2,1)S(1)} collective-permute-done((bf16[704,1152]{1,0:T(8,128)(2,1)S(1)}, bf16[704,1152]{1,0:T(8,128)(2,1)S(1)}, u32[]{:S(2)}, u32[]{:S(2)}) %collective-permute-start.1) | collective-permute-done | bytes 1622048 | tf_op jit(solution)/shard_map/ppermute | solution.py:15
  124.0 1.8 divide_convert_fusion.1
  125.8 1.6 convolution_multiply_fusion.1
  127.4 0.0 collective-permute-done.4
  127.4 0.3 add.61
  127.7 4.2 %collective-permute-start.5 = (f32[704,1152]{1,0:T(8,128)S(1)}, f32[704,1152]{1,0:T(8,128)S(1)}, u32[]{:S(2)}, u32[]{:S(2)}) collective-permute-start(f32[704,1152]{1,0:T(8,128)S(1)} %add.61), channel_id=1, source_target_pairs={{0,1},{1,2},{2,3},{3,4},{4,5},{5,6},{6,7},{7,8},{8,9},{9,10},{10,1... | collective-permute-start | bytes 9732104 | tf_op jit(solution)/shard_map/ppermute | solution.py:15
  132.0 0.1 collective-permute-start.2
  132.1 52.6 %collective-permute-done.2 = bf16[704,1152]{1,0:T(8,128)(2,1)S(1)} collective-permute-done((bf16[704,1152]{1,0:T(8,128)(2,1)S(1)}, bf16[704,1152]{1,0:T(8,128)(2,1)S(1)}, u32[]{:S(2)}, u32[]{:S(2)}) %collective-permute-start.2) | collective-permute-done | bytes 1622048 | tf_op jit(solution)/shard_map/ppermute | solution.py:15
  184.6 1.8 divide_convert_fusion
  186.4 1.6 convolution_multiply_fusion
  188.1 0.0 collective-permute-done.5
  188.1 0.3 add.62
  188.4 11.5 %collective-permute-start.6 = (f32[704,1152]{1,0:T(8,128)S(1)}, f32[704,1152]{1,0:T(8,128)S(1)}, u32[]{:S(2)}, u32[]{:S(2)}) collective-permute-start(f32[704,1152]{1,0:T(8,128)S(1)} %add.62), channel_id=1, source_target_pairs={{0,253},{1,254},{2,255},{3,0},{4,1},{5,2},{6,3},{7,4},{8,5},{9,6},... | collective-permute-start | bytes 9732104 | tf_op jit(solution)/shard_map/ppermute | solution.py:15
  199.9 1.6 fusion.2
  201.5 1.6 convolution_add_fusion.2
  203.1 1.6 convolution_add_fusion.1
  204.7 3.3 %fusion.1 = f32[704,1152]{1,0:T(8,128)} fusion(f32[704,1152]{1,0:T(8,128)S(1)} %convolution_add_fusion.1, bf16[704,704]{1,0:T(8,128)(2,1)S(1)} %divide_convert_fusion, bf16[704,1152]{1,0:T(8,128)(2,1)S(1)} %collective-permute-done.2, f32[]{:T(128)} %bitcast), kind=kOutput, calls=%fused_computation.6 | convolution fusion | flops 1143521280 | bytes 9101316 | tf_op jit(solution)/shard_map/dot_general | solution.py:35
  207.9 57.3 %collective-permute-done.6 = f32[704,1152]{1,0:T(8,128)S(1)} collective-permute-done((f32[704,1152]{1,0:T(8,128)S(1)}, f32[704,1152]{1,0:T(8,128)S(1)}, u32[]{:S(2)}, u32[]{:S(2)}) %collective-permute-start.6) | collective-permute-done | bytes 3244064 | tf_op jit(solution)/shard_map/ppermute | solution.py:15
  265.3 1.7 copy.9
Async XLA Ops:
  0.6 1.4 copy-start
  5.3 5.9 %copy-start.1 = (bf16[704,1152]{1,0:T(8,128)(2,1)S(1)}, bf16[704,1152]{1,0:T(8,128)(2,1)}, u32[]{:S(2)}) copy-start(bf16[704,1152]{1,0:T(8,128)(2,1)} %param.5) | copy-start | bytes 4866052
  6.9 58.7 %collective-permute-start.3 = (f32[704,1152]{1,0:T(8,128)S(1)}, f32[704,1152]{1,0:T(8,128)S(1)}, u32[]{:S(2)}, u32[]{:S(2)}) collective-permute-start(f32[704,1152]{1,0:T(8,128)S(1)} %convolution_multiply_fusion.3), channel_id=1, source_target_pairs={{0,1},{1,2},{2,3},{3,4},{4,5},{5,6},{6,7},{7,8},{8,9},{9,10},{10,1... | collective-permute-start | bytes 9732104 | tf_op jit(solution)/shard_map/ppermute | solution.py:15
  11.2 52.6 %collective-permute-start = (bf16[704,1152]{1,0:T(8,128)(2,1)S(1)}, bf16[704,1152]{1,0:T(8,128)(2,1)S(1)}, u32[]{:S(2)}, u32[]{:S(2)}) collective-permute-start(bf16[704,1152]{1,0:T(8,128)(2,1)S(1)} %copy-done.1), channel_id=1, source_target_pairs={{0,1},{1,2},{2,3},{3,4},{4,5},{5,6},{6,7},{7,8},{8,9},{9,10},{10,1... | collective-permute-start | bytes 4866056 | tf_op jit(solution)/shard_map/ppermute | solution.py:15
  67.3 60.2 %collective-permute-start.4 = (f32[704,1152]{1,0:T(8,128)S(1)}, f32[704,1152]{1,0:T(8,128)S(1)}, u32[]{:S(2)}, u32[]{:S(2)}) collective-permute-start(f32[704,1152]{1,0:T(8,128)S(1)} %fusion), channel_id=1, source_target_pairs={{0,1},{1,2},{2,3},{3,4},{4,5},{5,6},{6,7},{7,8},{8,9},{9,10},{10,1... | collective-permute-start | bytes 9732104 | tf_op jit(solution)/shard_map/ppermute | solution.py:15
  71.3 52.6 %collective-permute-start.1 = (bf16[704,1152]{1,0:T(8,128)(2,1)S(1)}, bf16[704,1152]{1,0:T(8,128)(2,1)S(1)}, u32[]{:S(2)}, u32[]{:S(2)}) collective-permute-start(bf16[704,1152]{1,0:T(8,128)(2,1)S(1)} %collective-permute-done), channel_id=1, source_target_pairs={{0,1},{1,2},{2,3},{3,4},{4,5},{5,6},{6,7},{7,8},{8,9},{9,10},{10,1... | collective-permute-start | bytes 4866056 | tf_op jit(solution)/shard_map/ppermute | solution.py:15
  127.7 60.3 %collective-permute-start.5 = (f32[704,1152]{1,0:T(8,128)S(1)}, f32[704,1152]{1,0:T(8,128)S(1)}, u32[]{:S(2)}, u32[]{:S(2)}) collective-permute-start(f32[704,1152]{1,0:T(8,128)S(1)} %add.61), channel_id=1, source_target_pairs={{0,1},{1,2},{2,3},{3,4},{4,5},{5,6},{6,7},{7,8},{8,9},{9,10},{10,1... | collective-permute-start | bytes 9732104 | tf_op jit(solution)/shard_map/ppermute | solution.py:15
  132.0 52.6 %collective-permute-start.2 = (bf16[704,1152]{1,0:T(8,128)(2,1)S(1)}, bf16[704,1152]{1,0:T(8,128)(2,1)S(1)}, u32[]{:S(2)}, u32[]{:S(2)}) collective-permute-start(bf16[704,1152]{1,0:T(8,128)(2,1)S(1)} %collective-permute-done.1), channel_id=1, source_target_pairs={{0,1},{1,2},{2,3},{3,4},{4,5},{5,6},{6,7},{7,8},{8,9},{9,10},{10,1... | collective-permute-start | bytes 4866056 | tf_op jit(solution)/shard_map/ppermute | solution.py:15
  188.4 76.9 %collective-permute-start.6 = (f32[704,1152]{1,0:T(8,128)S(1)}, f32[704,1152]{1,0:T(8,128)S(1)}, u32[]{:S(2)}, u32[]{:S(2)}) collective-permute-start(f32[704,1152]{1,0:T(8,128)S(1)} %add.62), channel_id=1, source_target_pairs={{0,253},{1,254},{2,255},{3,0},{4,1},{5,2},{6,3},{7,4},{8,5},{9,6},... | collective-permute-start | bytes 9732104 | tf_op jit(solution)/shard_map/ppermute | solution.py:15
where the time goes:
time: 270 us; the launch traced here: 267 us
  waiting for transfers between devices  215 us (80%)
  starting transfers between devices  24.3 us (9%)
  matrix products  23.1 us (9%)
    ppermute x7, waiting for transfers between devices, from_behind(): return lax.ppermute(value, axis, pairs)  215 us
    ppermute x7, starting transfers between devices, from_behind(): return lax.ppermute(value, axis, pairs)  24.3 us
    dot_general x4, matrix products, body(): lax.dot_general(images, text_block, (((1,), (1,)), ((), ())), preferred_e...  8.61 us
    dot_general x4, matrix products, body(): jnp.dot(weights, text_block, preferred_element_type=jnp.float32)  7.99 us
    dot_general x4, matrix products, body(): lax.dot_general(weights, images, (((0,), (0,)), ((), ())), preferred_elem...  6.47 us
  transfers between devices with their start and end apart: 7, of which 4 were waited for; matrix products, arithmetic and copies ran while one was open for 6% of the time, Pallas kernels for 0%

commit v1 on v0

v1 whole, which is shorter than its diff:
```python
import math

import jax
import jax.numpy as jnp
from jax import lax
from jax.experimental import pallas as pl
from jax.experimental.pallas import tpu as pltpu
from jax.sharding import PartitionSpec as P

CHUNKS = 4
X, Y, LOCAL, D1, D1F, EXTRA, TRANSIT, ZIN, D2, D2F = range(10)
F_LOCAL, F_P1, F_RELAY, F_MZ, F_Z, F_P2, F_M2, F_D1, F_D2 = range(9)


def kernel(ndp, x_ref, y_ref, scale_ref, bias_ref, img_ref, txt_ref, buf, acc, load_sem, out_sem, send_sem, recv_sem):
    rows, width = x_ref.shape
    part = rows // CHUNKS
    dp, tensor = lax.axis_index("dp"), lax.axis_index("tensor")
    core, xh, xl = lax.rem(tensor, 2), tensor // 2, lax.rem(dp, 2)
    is_a = core == xh
    is_z = xl == xh
    not_z = jnp.logical_not(is_z)
    is_b = jnp.logical_not(is_a)
    a = is_a.astype(jnp.int32)
    z = is_z.astype(jnp.int32)

    cut = (dp + 1 - 2 * xl, (1 - xh) * 2 + core)
    side = (dp + 1 - 2 * xl, xh * 2 + 1 - core)
    sibling = (dp, xh * 2 + 1 - core)

    def along_z(sign):
        return (lax.rem(dp + 2 * sign + ndp, ndp), tensor)

    z_extra = 1 - 2 * xh
    z_second = 2 * xh - 1
    first_src, second_src = 1 - xh, xh

    loads = [
        pltpu.make_async_copy(x_ref, buf.at[X], load_sem.at[0]),
        pltpu.make_async_copy(y_ref, buf.at[Y], load_sem.at[1]),
    ]
    for load in loads:
        load.start()
    mesh_id = dict(device_id_type=pl.DeviceIdType.MESH)
    barrier = pltpu.get_barrier_semaphore()
    for peer in (cut, side, sibling):
        pl.semaphore_signal(barrier, inc=1, device_id=peer, **mesh_id)

    @pl.when(is_z)
    def _():
        for sign in (1, -1):
            pl.semaphore_signal(barrier, inc=1, device_id=along_z(sign), **mesh_id)

    acc[...] = jnp.zeros_like(acc)
    for load in loads:
        load.wait()

    pl.semaphore_wait(barrier, 3 + 2 * z)

    def span(k):
        return pl.ds(pl.multiple_of(k * part, 16), part)

    def copy(flow, src, dst, peer, k):
        return pltpu.make_async_remote_copy(
            src_ref=buf.at[src, span(k)],
            dst_ref=buf.at[dst, span(k)],
            send_sem=send_sem.at[flow, k],
            recv_sem=recv_sem.at[dst, k],
            device_id=peer,
            **mesh_id,
        )

    def arrive(b, k):
        pltpu.make_async_copy(buf.at[b, span(k)], buf.at[b, span(k)], recv_sem.at[b, k]).wait()

    def sent(flow, k):
        pltpu.make_async_copy(buf.at[X, span(k)], buf.at[X, span(k)], send_sem.at[flow, k]).wait()

    second_from = jnp.where(is_z, ZIN, second_src)

    def each(body):
        lax.fori_loop(0, CHUNKS, lambda k, c: (body(k), c)[1], 0)

    @each
    def _(k):
        @pl.when(is_a)
        def _():
            copy(F_P1, first_src, TRANSIT, cut, k).start()

        @pl.when(is_b)
        def _():
            copy(F_P1, first_src, jnp.where(is_z, EXTRA, TRANSIT), side, k).start()

        @pl.when(is_z)
        def _():
            copy(F_Z, second_src, ZIN, along_z(z_second), k).start()

        @pl.when(jnp.logical_and(not_z, is_b))
        def _():
            copy(F_P2, second_from, D2, cut, k).start()

        copy(F_LOCAL, 1 - core, LOCAL, sibling, k).start()

    def relay_a(k):
        held = jnp.where(is_z, TRANSIT, EXTRA)
        arrive(held, k)
        copy(F_RELAY, held, D1, cut, k).start()

        @pl.when(is_z)
        def _():
            copy(F_MZ, TRANSIT, EXTRA, along_z(z_extra), k).start()

    def relay_b(k):
        arrive(TRANSIT, k)
        copy(F_RELAY, TRANSIT, D1, side, k).start()

        @pl.when(is_z)
        def _():
            arrive(ZIN, k)
            copy(F_P2, ZIN, D2, cut, k).start()

    def second_a(k):
        @pl.when(is_z)
        def _():
            arrive(ZIN, k)

        copy(F_P2, second_from, D2, cut, k).start()
        copy(F_M2, second_from, EXTRA, side, k).start()

    factor = scale_ref[0] / math.sqrt(width)
    bias = bias_ref[0]

    def weigh(s, b, k, own):
        block = buf[b, span(k), :]
        logits = lax.dot_general(buf[s], block, (((1,), (1,)), ((), ())), preferred_element_type=jnp.float32)
        weights = jax.nn.sigmoid(factor * logits + bias)
        row = lax.broadcasted_iota(jnp.int32, weights.shape, 0)
        column = lax.broadcasted_iota(jnp.int32, weights.shape, 1)
        shift = jnp.where(own, k * part, -2 * rows)
        weights = weights - (row == column + shift).astype(jnp.float32)
        acc[s] += jnp.dot(weights.astype(jnp.bfloat16), block, preferred_element_type=jnp.float32)

    def scale_out(s, copy_out):
        for k in range(CHUNKS):
            tile = pl.ds(k * part, part)
            acc[s, tile, :] = acc[s, tile, :] * factor
            copy_out(s, k, True)

    def out_copy(s, k, start):
        tile = pl.ds(k * part, part)

        @pl.when(s == 0)
        def _():
            c = pltpu.make_async_copy(acc.at[0, tile], img_ref.at[tile], out_sem.at[0, k])
            c.start() if start else c.wait()

        @pl.when(s == 1)
        def _():
            c = pltpu.make_async_copy(acc.at[1, tile], txt_ref.at[tile], out_sem.at[1, k])
            c.start() if start else c.wait()

    def step(t, carry):
        @pl.when(jnp.logical_and(is_a, jnp.logical_and(lax.rem(t, 3) == 0, jnp.logical_and(t >= 3, t <= 12))))
        def _():
            relay_a(t // 3 - 1)

        @pl.when(jnp.logical_and(is_b, jnp.logical_or(t == 8, jnp.logical_and(lax.rem(t, 2) == 0, jnp.logical_and(t >= 12, t <= 16)))))
        def _():
            relay_b(jnp.where(t == 8, 0, (t - 10) // 2))

        @pl.when(jnp.logical_and(is_a, t == 20))
        def _():
            each(second_a)

        @pl.when(t == 28)
        def _():
            scale_out(1 - xh, out_copy)

        u1, u2 = t - 12, t - 20
        even = lax.rem(t, 2) == 0
        first, second = 1 - xh, xh
        k = jnp.where(t < 12, lax.rem(t, 4), jnp.where(t < 20, u1 // 2, jnp.where(t < 28, u2 // 2, t - 28)))
        b = jnp.where(t < 4, Y, jnp.where(t < 8, X, jnp.where(t < 12, LOCAL,
            jnp.where(t < 20, jnp.where(even, D2F - a, D1F - a),
            jnp.where(t < 28, jnp.where(even, D1 + a, EXTRA), D2 + a)))))
        s = jnp.where(t < 4, 0, jnp.where(t < 8, 1, jnp.where(t < 12, jnp.where(is_a, first, second),
            jnp.where(t < 20, jnp.where(even, second, first),
            jnp.where(t < 28, jnp.where(even, first, jnp.where(is_a, second, first)), second)))))
        seen = jnp.logical_or(t < 8, jnp.logical_and(b == EXTRA, jnp.logical_and(is_a, not_z)))

        @pl.when(jnp.logical_not(seen))
        def _():
            arrive(b, k)

        @pl.when(b == D1)
        def _():
            copy(F_D1, D1, D1F, sibling, k).start()

        @pl.when(b == D2)
        def _():
            copy(F_D2, D2, D2F, sibling, k).start()

        weigh(s, b, k, t < 8)
        return carry

    lax.fori_loop(0, 8 * CHUNKS, step, 0)
    scale_out(xh, out_copy)

    @each
    def _(k):
        for flow in (F_LOCAL, F_P1, F_RELAY, F_P2, F_D1, F_D2):
            sent(flow, k)

        @pl.when(is_a)
        def _():
            sent(F_M2, k)

        @pl.when(is_z)
        def _():
            sent(F_Z, k)

        @pl.when(jnp.logical_and(is_z, is_a))
        def _():
            sent(F_MZ, k)

    for s in range(2):
        for k in range(CHUNKS):
            out_copy(s, k, False)


def body(images, texts, logit_scale, logit_bias):
    import functools

    rows, width = images.shape
    any_spec = pl.BlockSpec(memory_space=pl.ANY)
    smem = pl.BlockSpec(memory_space=pltpu.SMEM)
    out = jax.ShapeDtypeStruct((rows, width), jnp.float32)
    return pl.pallas_call(
        functools.partial(kernel, lax.axis_size("dp")),
        out_shape=(out, out),
        in_specs=[any_spec, any_spec, smem, smem],
        out_specs=(any_spec, any_spec),
        scratch_shapes=[
            pltpu.VMEM((10, rows, width), jnp.bfloat16),
            pltpu.VMEM((2, rows, width), jnp.float32),
            pltpu.SemaphoreType.DMA((2,)),
            pltpu.SemaphoreType.DMA((2, CHUNKS)),
            pltpu.SemaphoreType.DMA((9, CHUNKS)),
            pltpu.SemaphoreType.DMA((10, CHUNKS)),
        ],
        compiler_params=pltpu.CompilerParams(
            collective_id=0, has_side_effects=True, vmem_limit_bytes=60 << 20
        ),
        cost_estimate=pl.CostEstimate(
            flops=32 * rows * rows * width, bytes_accessed=12 * rows * width, transcendentals=8 * rows * rows
        ),
        name="pairs",
    )(images, texts, logit_scale, logit_bias)


def solution(mesh):
    in_specs = (P(("dp", "tensor"), None), P(("dp", "tensor"), None), P(), P())
    out_specs = (P(("dp", "tensor"), None), P(("dp", "tensor"), None))
    return jax.shard_map(body, mesh=mesh, in_specs=in_specs, out_specs=out_specs, check_vma=False)
```

time: 270 us -> 109 us (0.40)
  the two profiles are of different devices: /device:TPU:1 before, /device:TPU:2 now
where the time goes in v1:
time: 109 us
  Pallas kernels  101 us (93%)
  local copies, waits for them, and re-layouts  5.67 us (5%)
  between operations  1.94 us (2%)
    pallas_call x1, Pallas kernels, body(): pl.pallas_call(functools.partial(kernel, lax.axis_size('dp')), out_shape=...  101 us
    unnamed x4, local copies, waits for them, and re-layouts  5.67 us

profile of v1, /device:TPU:2, one launch (start us, length us, event | category | flops | bytes accessed | tf_op | source)
XLA Modules:
  0.0 109.1 jit_solution(17963892485412291251)
XLA Ops:
  1.9 101.5 %pairs.1 = (f32[704,1152]{1,0:T(8,128)}, f32[704,1152]{1,0:T(8,128)}) custom-call(bf16[704,1152]{1,0:T(8,128)(2,1)} %x_ref.1, bf16[704,1152]{1,0:T(8,128)(2,1)} %y_ref.1, f32[1]{0:T(128)S(6)} %copy.8.scale_ref, f32[1]{0:T(128)S(6)} %copy.9.bias_ref), custom_call_target="tpu_custom_call" | custom-call | flops 18270388224 | bytes 9732096 | tf_op jit(solution)/shard_map/pairs/pallas_call | solution.py:238
  103.4 0.0 copy-start
  103.4 4.0 %copy.10 = f32[704,1152]{1,0:T(8,128)} copy(f32[704,1152]{1,0:T(8,128)} %get-tuple-element.4) | data formatting | bytes 6488064
  107.4 0.0 copy-done
  107.4 1.7 %copy.11 = f32[704,1152]{1,0:T(8,128)} copy(f32[704,1152]{1,0:T(8,128)S(1)} %copy-done) | data formatting | bytes 6488064
Async XLA Ops:
  103.4 4.0 %copy-start = (f32[704,1152]{1,0:T(8,128)S(1)}, f32[704,1152]{1,0:T(8,128)}, u32[]{:S(2)}) copy-start(f32[704,1152]{1,0:T(8,128)} %get-tuple-element.5) | copy-start | bytes 9732100

commit v2 on v1

--- a/solution.py
+++ b/solution.py
@@ -1,3 +1,4 @@
+import functools
 import math
 
 import jax
@@ -12,7 +13,7 @@
 F_LOCAL, F_P1, F_RELAY, F_MZ, F_Z, F_P2, F_M2, F_D1, F_D2 = range(9)
 
 
-def kernel(ndp, x_ref, y_ref, scale_ref, bias_ref, img_ref, txt_ref, buf, acc, load_sem, out_sem, send_sem, recv_sem):
+def kernel(ndp, x_ref, y_ref, scale_ref, bias_ref, acc, buf, load_sem, send_sem, recv_sem):
     rows, width = x_ref.shape
     part = rows // CHUNKS
     dp, tensor = lax.axis_index("dp"), lax.axis_index("tensor")
@@ -130,81 +131,113 @@
     factor = scale_ref[0] / math.sqrt(width)
     bias = bias_ref[0]
 
-    def weigh(s, b, k, own):
-        block = buf[b, span(k), :]
+    def weigh(s, b, rows_of, own):
+        block = buf[b, rows_of, :]
         logits = lax.dot_general(buf[s], block, (((1,), (1,)), ((), ())), preferred_element_type=jnp.float32)
         weights = jax.nn.sigmoid(factor * logits + bias)
-        row = lax.broadcasted_iota(jnp.int32, weights.shape, 0)
-        column = lax.broadcasted_iota(jnp.int32, weights.shape, 1)
-        shift = jnp.where(own, k * part, -2 * rows)
-        weights = weights - (row == column + shift).astype(jnp.float32)
+        if own is not None:
+            row = lax.broadcasted_iota(jnp.int32, weights.shape, 0)
+            column = lax.broadcasted_iota(jnp.int32, weights.shape, 1)
+            weights = weights - (row == column + jnp.where(own, 0, rows)).astype(jnp.float32)
         acc[s] += jnp.dot(weights.astype(jnp.bfloat16), block, preferred_element_type=jnp.float32)
 
-    def scale_out(s, copy_out):
-        for k in range(CHUNKS):
-            tile = pl.ds(k * part, part)
-            acc[s, tile, :] = acc[s, tile, :] * factor
-            copy_out(s, k, True)
-
-    def out_copy(s, k, start):
-        tile = pl.ds(k * part, part)
-
-        @pl.when(s == 0)
-        def _():
-            c = pltpu.make_async_copy(acc.at[0, tile], img_ref.at[tile], out_sem.at[0, k])
-            c.start() if start else c.wait()
-
-        @pl.when(s == 1)
-        def _():
-            c = pltpu.make_async_copy(acc.at[1, tile], txt_ref.at[tile], out_sem.at[1, k])
-            c.start() if start else c.wait()
-
-    def step(t, carry):
-        @pl.when(jnp.logical_and(is_a, jnp.logical_and(lax.rem(t, 3) == 0, jnp.logical_and(t >= 3, t <= 12))))
-        def _():
-            relay_a(t // 3 - 1)
-
-        @pl.when(jnp.logical_and(is_b, jnp.logical_or(t == 8, jnp.logical_and(lax.rem(t, 2) == 0, jnp.logical_and(t >= 12, t <= 16)))))
-        def _():
-            relay_b(jnp.where(t == 8, 0, (t - 10) // 2))
-
-        @pl.when(jnp.logical_and(is_a, t == 20))
-        def _():
-            each(second_a)
-
-        @pl.when(t == 28)
-        def _():
-            scale_out(1 - xh, out_copy)
-
-        u1, u2 = t - 12, t - 20
-        even = lax.rem(t, 2) == 0
+    def both(b, forward_flow):
+        def one(k):
+            arrive(b, k)
+            copy(forward_flow, b, b + 1, sibling, k).start()
+
+        return one
+
+    def at(u, cond, number):
+        return pl.when(jnp.logical_and(u == number, cond))
+
+    def unit(u, carry):
+        @at(u, is_a, 1)
+        def _():
+            relay_a(0)
+
+        @at(u, is_a, 2)
+        def _():
+            relay_a(1)
+
+        @at(u, is_b, 2)
+        def _():
+            relay_b(0)
+
+        @pl.when(u == 2)
+        def _():
+            each(lambda k: arrive(LOCAL, k))
+
+        @at(u, is_a, 3)
+        def _():
+            relay_a(2)
+            both(D2, F_D2)(0)
+            relay_a(3)
+
+            @pl.when(not_z)
+            def _():
+                each(second_a)
+
+            both(D2, F_D2)(1)
+
+            @pl.when(is_z)
+            def _():
+                each(lambda k: arrive(EXTRA, k))
+
+        @at(u, is_b, 3)
+        def _():
+            relay_b(1)
+            relay_b(2)
+            relay_b(3)
+            each(lambda k: arrive(D2F, k))
+
+        @at(u, is_a, 4)
+        def _():
+            @pl.when(is_z)
+            def _():
+                each(second_a)
+
+            both(D2, F_D2)(2)
+            both(D2, F_D2)(3)
+
+        @at(u, is_b, 4)
+        def _():
+            each(lambda k: arrive(D1F, k))
+
+        @pl.when(u == 5)
+        def _():
+            each(both(D1, F_D1))
+
+        @at(u, is_a, 6)
+        def _():
+            each(lambda k: arrive(D1F, k))
+
+        @at(u, is_b, 6)
+        def _():
+            each(lambda k: arrive(EXTRA, k))
+
         first, second = 1 - xh, xh
-        k = jnp.where(t < 12, lax.rem(t, 4), jnp.where(t < 20, u1 // 2, jnp.where(t < 28, u2 // 2, t - 28)))
-        b = jnp.where(t < 4, Y, jnp.where(t < 8, X, jnp.where(t < 12, LOCAL,
-            jnp.where(t < 20, jnp.where(even, D2F - a, D1F - a),
-            jnp.where(t < 28, jnp.where(even, D1 + a, EXTRA), D2 + a)))))
-        s = jnp.where(t < 4, 0, jnp.where(t < 8, 1, jnp.where(t < 12, jnp.where(is_a, first, second),
-            jnp.where(t < 20, jnp.where(even, second, first),
-            jnp.where(t < 28, jnp.where(even, first, jnp.where(is_a, second, first)), second)))))
-        seen = jnp.logical_or(t < 8, jnp.logical_and(b == EXTRA, jnp.logical_and(is_a, not_z)))
-
-        @pl.when(jnp.logical_not(seen))
-        def _():
-            arrive(b, k)
-
-        @pl.when(b == D1)
-        def _():
-            copy(F_D1, D1, D1F, sibling, k).start()
-
-        @pl.when(b == D2)
-        def _():
-            copy(F_D2, D2, D2F, sibling, k).start()
-
-        weigh(s, b, k, t < 8)
+        b = jnp.where(u == 0, Y, jnp.where(u == 1, X, jnp.where(u == 2, LOCAL, jnp.where(u == 3,
+            jnp.where(is_a, EXTRA, D2F), jnp.where(u == 4, jnp.where(is_a, D2, D1F),
+            jnp.where(u == 5, D1, jnp.where(is_a, D1F, EXTRA)))))))
+        in_first = jnp.where(u == 2, is_a, jnp.where(u == 3, False, jnp.where(u == 4, is_b, True)))
+        s = jnp.where(u == 0, 0, jnp.where(u == 1, 1, jnp.where(in_first, first, second)))
+        weigh(s, b, slice(None), u < 2)
         return carry
 
-    lax.fori_loop(0, 8 * CHUNKS, step, 0)
-    scale_out(xh, out_copy)
+    lax.fori_loop(0, 7, unit, 0)
+
+    @each
+    def _(k):
+        @pl.when(is_a)
+        def _():
+            arrive(D2F, k)
+
+        @pl.when(is_b)
+        def _():
+            both(D2, F_D2)(k)
+
+        weigh(xh, D2 + a, span(k), None)
 
     @each
     def _(k):
@@ -223,39 +256,32 @@
         def _():
             sent(F_MZ, k)
 
-    for s in range(2):
-        for k in range(CHUNKS):
-            out_copy(s, k, False)
-
 
 def body(images, texts, logit_scale, logit_bias):
-    import functools
-
     rows, width = images.shape
-    any_spec = pl.BlockSpec(memory_space=pl.ANY)
+    hbm = pl.BlockSpec(memory_space=pltpu.HBM)
     smem = pl.BlockSpec(memory_space=pltpu.SMEM)
-    out = jax.ShapeDtypeStruct((rows, width), jnp.float32)
-    return pl.pallas_call(
+    factor = logit_scale[0] / math.sqrt(width)
+    total = pl.pallas_call(
         functools.partial(kernel, lax.axis_size("dp")),
-        out_shape=(out, out),
-        in_specs=[any_spec, any_spec, smem, smem],
-        out_specs=(any_spec, any_spec),
+        out_shape=pltpu.VMEM((2, rows, width), jnp.float32),
+        in_specs=[hbm, hbm, smem, smem],
+        out_specs=pl.BlockSpec(memory_space=pltpu.VMEM),
         scratch_shapes=[
             pltpu.VMEM((10, rows, width), jnp.bfloat16),
-            pltpu.VMEM((2, rows, width), jnp.float32),
             pltpu.SemaphoreType.DMA((2,)),
-            pltpu.SemaphoreType.DMA((2, CHUNKS)),
             pltpu.SemaphoreType.DMA((9, CHUNKS)),
             pltpu.SemaphoreType.DMA((10, CHUNKS)),
         ],
         compiler_params=pltpu.CompilerParams(
-            collective_id=0, has_side_effects=True, vmem_limit_bytes=60 << 20
+            collective_id=0, has_side_effects=True, vmem_limit_bytes=57 << 20
         ),
         cost_estimate=pl.CostEstimate(
             flops=32 * rows * rows * width, bytes_accessed=12 * rows * width, transcendentals=8 * rows * rows
         ),
         name="pairs",
     )(images, texts, logit_scale, logit_bias)
+    return (factor * total[0], factor * total[1])
 
 
 def solution(mesh):

time: 109 us -> 92.7 us (0.85)
  the two profiles are of different devices: /device:TPU:2 before, /device:TPU:1 now
where the time goes in v2:
time: 92.7 us; the launch traced here: 92.6 us
  Pallas kernels  87.5 us (94%)
  other arithmetic  3.19 us (3%)
  between operations  1.93 us (2%)
    pallas_call x1, Pallas kernels, body(): pl.pallas_call(functools.partial(kernel, lax.axis_size('dp')), out_shape=...  87.5 us
    mul x1, other arithmetic, body(): return (factor * total[0], factor * total[1])  3.19 us

profile of v2, /device:TPU:1, one launch (start us, length us, event | category | flops | bytes accessed | tf_op | source)
XLA Modules:
  0.0 92.6 jit_solution(13662699069411302690)
XLA Ops:
  1.9 87.5 %pairs.1 = f32[2,704,1152]{2,1,0:T(8,128)S(1)} custom-call(bf16[704,1152]{1,0:T(8,128)(2,1)} %x_ref.1, bf16[704,1152]{1,0:T(8,128)(2,1)} %y_ref.1, f32[1]{0:T(128)S(6)} %copy.6.scale_ref, f32[1]{0:T(128)S(6)} %copy.7.bias_ref), custom_call_target="tpu_custom_call" | custom-call | flops 18270388224 | bytes 9732096 | tf_op jit(solution)/shard_map/pairs/pallas_call | solution.py:265
  89.4 3.2 %multiply_bitcast_fusion = (f32[704,1152]{1,0:T(8,128)}, f32[704,1152]{1,0:T(8,128)}) fusion(f32[2,704,1152]{2,1,0:T(8,128)S(1)} %pairs.1, f32[]{:T(128)} %bitcast), kind=kLoop, calls=%fused_computation | loop fusion | flops 1622016 | bytes 12976132 | tf_op jit(solution)/shard_map/mul | solution.py:284

commit v3 on v2

--- a/solution.py
+++ b/solution.py
@@ -9,11 +9,12 @@
 from jax.sharding import PartitionSpec as P
 
 CHUNKS = 4
+TILES = 4
 X, Y, LOCAL, D1, D1F, EXTRA, TRANSIT, ZIN, D2, D2F = range(10)
 F_LOCAL, F_P1, F_RELAY, F_MZ, F_Z, F_P2, F_M2, F_D1, F_D2 = range(9)
 
 
-def kernel(ndp, x_ref, y_ref, scale_ref, bias_ref, acc, buf, load_sem, send_sem, recv_sem):
+def kernel(ndp, x_ref, y_ref, scale_ref, bias_ref, acc, buf, load_sem, send_sem, recv_sem, ready):
     rows, width = x_ref.shape
     part = rows // CHUNKS
     dp, tensor = lax.axis_index("dp"), lax.axis_index("tensor")
@@ -50,13 +51,17 @@
     @pl.when(is_z)
     def _():
         for sign in (1, -1):
-            pl.semaphore_signal(barrier, inc=1, device_id=along_z(sign), **mesh_id)
+            pl.semaphore_signal(barrier, inc=1, device_id=(along_z(sign)[0], xh * 2 + 1 - xh), **mesh_id)
 
     acc[...] = jnp.zeros_like(acc)
     for load in loads:
         load.wait()
 
-    pl.semaphore_wait(barrier, 3 + 2 * z)
+    pl.semaphore_wait(barrier, 3 + 4 * z * (1 - a))
+
+    @pl.when(jnp.logical_and(is_z, is_b))
+    def _():
+        pl.semaphore_signal(ready, inc=1, device_id=sibling, **mesh_id)
 
     def span(k):
         return pl.ds(pl.multiple_of(k * part, 16), part)
@@ -82,6 +87,9 @@
     def each(body):
         lax.fori_loop(0, CHUNKS, lambda k, c: (body(k), c)[1], 0)
 
+    def send_z(k):
+        copy(F_Z, second_src, ZIN, along_z(z_second), k).start()
+
     @each
     def _(k):
         @pl.when(is_a)
@@ -92,9 +100,9 @@
         def _():
             copy(F_P1, first_src, jnp.where(is_z, EXTRA, TRANSIT), side, k).start()
 
-        @pl.when(is_z)
-        def _():
-            copy(F_Z, second_src, ZIN, along_z(z_second), k).start()
+        @pl.when(jnp.logical_and(is_z, is_b))
+        def _():
+            send_z(k)
 
         @pl.when(jnp.logical_and(not_z, is_b))
         def _():
@@ -154,6 +162,11 @@
     def unit(u, carry):
         @at(u, is_a, 1)
         def _():
+            @pl.when(is_z)
+            def _():
+                pl.semaphore_wait(ready, 1)
+                each(send_z)
+
             relay_a(0)
 
         @at(u, is_a, 2)
@@ -227,6 +240,8 @@
 
     lax.fori_loop(0, 7, unit, 0)
 
+    acc[1 - xh] = acc[1 - xh] * factor
+
     @each
     def _(k):
         @pl.when(is_a)
@@ -237,7 +252,9 @@
         def _():
             both(D2, F_D2)(k)
 
-        weigh(xh, D2 + a, span(k), None)
+        @pl.when(k < CHUNKS - 1)
+        def _():
+            weigh(xh, D2 + a, span(k), None)
 
     @each
     def _(k):
@@ -257,31 +274,85 @@
             sent(F_MZ, k)
 
 
+def finish(acc, buf, scale_ref, bias_ref, img_ref, txt_ref, result, sem):
+    rows, width = img_ref.shape
+    part = rows // CHUNKS
+    tile = rows // TILES
+    tensor = lax.axis_index("tensor")
+    core, xh = lax.rem(tensor, 2), tensor // 2
+    factor = scale_ref[0] / math.sqrt(width)
+    bias = bias_ref[0]
+
+    def write(src, dst, number):
+        return pltpu.make_async_copy(src, dst, sem.at[number])
+
+    def first(start):
+        for s, ref in ((0, img_ref), (1, txt_ref)):
+            @pl.when(xh == 1 - s)
+            def _():
+                c = write(acc.at[s], ref, 0)
+                c.start() if start else c.wait()
+
+    def second(m, start):
+        span = pl.ds(m * tile, tile)
+        for s, ref in ((0, img_ref), (1, txt_ref)):
+            @pl.when(xh == s)
+            def _():
+                c = write(result.at[span], ref.at[span], 1 + m)
+                c.start() if start else c.wait()
+
+    first(True)
+    block = buf[D2 + (core == xh).astype(jnp.int32), rows - part :, :]
+    for m in range(TILES):
+        span = pl.ds(m * tile, tile)
+        logits = lax.dot_general(buf[xh, span, :], block, (((1,), (1,)), ((), ())), preferred_element_type=jnp.float32)
+        weights = jax.nn.sigmoid(factor * logits + bias).astype(jnp.bfloat16)
+        result[span, :] = factor * (acc[xh, span, :] + jnp.dot(weights, block, preferred_element_type=jnp.float32))
+        second(m, True)
+    first(False)
+    for m in range(TILES):
+        second(m, False)
+
+
 def body(images, texts, logit_scale, logit_bias):
     rows, width = images.shape
     hbm = pl.BlockSpec(memory_space=pltpu.HBM)
     smem = pl.BlockSpec(memory_space=pltpu.SMEM)
-    factor = logit_scale[0] / math.sqrt(width)
-    total = pl.pallas_call(
+    vmem = pl.BlockSpec(memory_space=pltpu.VMEM)
+    out = jax.ShapeDtypeStruct((rows, width), jnp.float32)
+    total, blocks = pl.pallas_call(
         functools.partial(kernel, lax.axis_size("dp")),
-        out_shape=pltpu.VMEM((2, rows, width), jnp.float32),
+        out_shape=(pltpu.VMEM((2, rows, width), jnp.float32), pltpu.VMEM((10, rows, width), jnp.bfloat16)),
         in_specs=[hbm, hbm, smem, smem],
-        out_specs=pl.BlockSpec(memory_space=pltpu.VMEM),
+        out_specs=(vmem, vmem),
         scratch_shapes=[
-            pltpu.VMEM((10, rows, width), jnp.bfloat16),
             pltpu.SemaphoreType.DMA((2,)),
             pltpu.SemaphoreType.DMA((9, CHUNKS)),
             pltpu.SemaphoreType.DMA((10, CHUNKS)),
+            pltpu.SemaphoreType.REGULAR,
         ],
         compiler_params=pltpu.CompilerParams(
-            collective_id=0, has_side_effects=True, vmem_limit_bytes=57 << 20
+            collective_id=0, has_side_effects=True, vmem_limit_bytes=41 << 20
         ),
         cost_estimate=pl.CostEstimate(
             flops=32 * rows * rows * width, bytes_accessed=12 * rows * width, transcendentals=8 * rows * rows
         ),
         name="pairs",
     )(images, texts, logit_scale, logit_bias)
-    return (factor * total[0], factor * total[1])
+    return pl.pallas_call(
+        finish,
+        out_shape=(out, out),
+        in_specs=[vmem, vmem, smem, smem],
+        out_specs=(hbm, hbm),
+        scratch_shapes=[pltpu.VMEM((rows, width), jnp.float32), pltpu.SemaphoreType.DMA((1 + TILES,))],
+        compiler_params=pltpu.CompilerParams(vmem_limit_bytes=41 << 20),
+        name="finish",
+    )(
+        pltpu.with_memory_space_constraint(total, pltpu.VMEM),
+        pltpu.with_memory_space_constraint(blocks, pltpu.VMEM),
+        logit_scale,
+        logit_bias,
+    )
 
 
 def solution(mesh):

time: 92.7 us -> 89.4 us (0.964)
  other arithmetic: 3.19 us -> 0 us
    mul x1 -> x0, other arithmetic: 3.19 us -> none  [body(): return (factor * total[0], factor * total[1])]
    pallas_call x1, Pallas kernels: 87.5 us -> 84.3 us  [body(): pl.pallas_call(functools.partial(kernel, lax.axis_size('dp')), out_shape=...]
    pallas_call x0 -> x1, Pallas kernels: none -> 2.8 us  [body(): pl.pallas_call(finish, out_shape=(out, out), in_specs=[vmem, vmem, smem,...]
where the time goes in v3:
time: 89.4 us; the launch traced here: 89.1 us
  Pallas kernels  87.1 us (97%)
  between operations  1.93 us (2%)
    pallas_call x1, Pallas kernels, body(): pl.pallas_call(functools.partial(kernel, lax.axis_size('dp')), out_shape=...  84.3 us
    pallas_call x1, Pallas kernels, body(): pl.pallas_call(finish, out_shape=(out, out), in_specs=[vmem, vmem, smem,...  2.8 us

profile of v3, /device:TPU:1, one launch (start us, length us, event | category | flops | bytes accessed | tf_op | source)
XLA Modules:
  0.0 89.1 jit_solution(3944676654310052222)
XLA Ops:
  1.9 84.3 %pairs.1 = (f32[2,704,1152]{2,1,0:T(8,128)S(1)}, bf16[10,704,1152]{2,1,0:T(8,128)(2,1)S(1)}) custom-call(bf16[704,1152]{1,0:T(8,128)(2,1)} %x_ref.1, bf16[704,1152]{1,0:T(8,128)(2,1)} %y_ref.1, f32[1]{0:T(128)S(6)} %copy.6.scale_ref, f32[1]{0:T(128)S(6)} %copy.7.bias_ref), custom_call_target="tpu_custom_call" | custom-call | flops 18270388224 | bytes 9732096 | tf_op jit(solution)/shard_map/pairs/pallas_call | solution.py:323
  86.3 2.8 %finish.1 = (f32[704,1152]{1,0:T(8,128)}, f32[704,1152]{1,0:T(8,128)}) custom-call(f32[2,704,1152]{2,1,0:T(8,128)S(1)} %get-tuple-element.4.acc, bf16[10,704,1152]{2,1,0:T(8,128)(2,1)S(1)} %get-tuple-element.5.buf, f32[1]{0:T(128)S(6)} %copy.6.scale_ref, f32[1]{0:T(128)S(6)} %copy.7.bias_ref), custom_call_target="tpu_custom_call" | custom-call | tf_op jit(solution)/shard_map/finish/pallas_call | solution.py:342

commit v4 on v3

--- a/solution.py
+++ b/solution.py
@@ -123,10 +123,9 @@
         arrive(TRANSIT, k)
         copy(F_RELAY, TRANSIT, D1, side, k).start()
 
-        @pl.when(is_z)
-        def _():
-            arrive(ZIN, k)
-            copy(F_P2, ZIN, D2, cut, k).start()
+    def second_b(k):
+        arrive(ZIN, k)
+        copy(F_P2, ZIN, D2, cut, k).start()
 
     def second_a(k):
         @pl.when(is_z)
@@ -139,14 +138,14 @@
     factor = scale_ref[0] / math.sqrt(width)
     bias = bias_ref[0]
 
-    def weigh(s, b, rows_of, own):
+    def weigh(s, b, rows_of, own, offset=0):
         block = buf[b, rows_of, :]
         logits = lax.dot_general(buf[s], block, (((1,), (1,)), ((), ())), preferred_element_type=jnp.float32)
         weights = jax.nn.sigmoid(factor * logits + bias)
         if own is not None:
             row = lax.broadcasted_iota(jnp.int32, weights.shape, 0)
             column = lax.broadcasted_iota(jnp.int32, weights.shape, 1)
-            weights = weights - (row == column + jnp.where(own, 0, rows)).astype(jnp.float32)
+            weights = weights - (row == column + jnp.where(own, offset, rows)).astype(jnp.float32)
         acc[s] += jnp.dot(weights.astype(jnp.bfloat16), block, preferred_element_type=jnp.float32)
 
     def both(b, forward_flow):
@@ -156,90 +155,214 @@
 
         return one
 
-    def at(u, cond, number):
-        return pl.when(jnp.logical_and(u == number, cond))
+    forward_1, forward_2 = both(D1, F_D1), both(D2, F_D2)
+
+    def arrive_half(b, h):
+        for k in range(h * CHUNKS // 2, (h + 1) * CHUNKS // 2):
+            arrive(b, k)
+
+    def before(cond, number):
+        return lambda body: plans.append((cond, number, body))
+
+    plans = []
+
+    a_z, b_z = jnp.logical_and(is_a, is_z), jnp.logical_and(is_b, is_z)
+    b_n = jnp.logical_and(is_b, not_z)
+
+    @before(a_z, 2)
+    def _():
+        pl.semaphore_wait(ready, 1)
+        each(send_z)
+
+    @before(is_a, 2)
+    def _():
+        relay_a(0)
+
+    @before(is_a, 4)
+    def _():
+        relay_a(1)
+
+    @before(is_b, 4)
+    def _():
+        relay_b(0)
+
+    @before(True, 4)
+    def _():
+        each(lambda k: arrive(LOCAL, k))
+
+    @before(b_z, 5)
+    def _():
+        second_b(0)
+
+    @before(is_a, 6)
+    def _():
+        relay_a(2)
+        relay_a(3)
+
+    @before(jnp.logical_and(is_a, not_z), 6)
+    def _():
+        each(second_a)
+
+    @before(is_a, 6)
+    def _():
+        forward_1(0)
+        forward_1(1)
+
+    @before(b_n, 6)
+    def _():
+        relay_b(1)
+        relay_b(2)
+        relay_b(3)
+
+    @before(b_z, 6)
+    def _():
+        relay_b(1)
+        second_b(1)
+        relay_b(2)
+        relay_b(3)
+        second_b(2)
+
+    @before(is_b, 6)
+    def _():
+        arrive_half(D1F, 0)
+
+    @before(a_z, 7)
+    def _():
+        arrive_half(EXTRA, 0)
+
+    @before(is_a, 7)
+    def _():
+        forward_2(0)
+
+    @before(b_z, 7)
+    def _():
+        arrive_half(EXTRA, 0)
+
+    @before(b_n, 7)
+    def _():
+        arrive_half(D2F, 0)
+
+    @before(a_z, 8)
+    def _():
+        second_a(0)
+        second_a(1)
+
+    @before(is_a, 8)
+    def _():
+        forward_2(1)
+
+    @before(b_z, 8)
+    def _():
+        second_b(3)
+        arrive_half(D2F, 0)
+
+    @before(b_n, 8)
+    def _():
+        arrive_half(D1F, 1)
+
+    @before(a_z, 9)
+    def _():
+        arrive_half(EXTRA, 1)
+        second_a(2)
+
+    @before(b_z, 9)
+    def _():
+        arrive_half(EXTRA, 1)
+
+    @before(b_n, 9)
+    def _():
+        arrive_half(D2F, 1)
+
+    @before(a_z, 10)
+    def _():
+        second_a(3)
+
+    @before(is_a, 10)
+    def _():
+        forward_1(2)
+
+    @before(is_a, 10)
+    def _():
+        forward_2(2)
+        forward_1(3)
+
+    @before(b_z, 10)
+    def _():
+        arrive_half(D1F, 1)
+
+    @before(b_n, 10)
+    def _():
+        forward_1(0)
+        forward_1(1)
+
+    @before(is_a, 11)
+    def _():
+        forward_2(3)
+
+    @before(b_z, 11)
+    def _():
+        forward_1(0)
+        forward_1(1)
+
+    @before(b_n, 11)
+    def _():
+        arrive_half(EXTRA, 0)
+
+    @before(is_a, 12)
+    def _():
+        arrive_half(D1F, 0)
+
+    @before(b_z, 12)
+    def _():
+        arrive_half(D2F, 1)
+
+    @before(b_n, 12)
+    def _():
+        forward_1(2)
+        forward_1(3)
+
+    @before(is_a, 13)
+    def _():
+        arrive_half(D1F, 1)
+
+    @before(b_z, 13)
+    def _():
+        forward_1(2)
+        forward_1(3)
+
+    @before(b_n, 13)
+    def _():
+        arrive_half(EXTRA, 1)
+
+    first, second = 1 - xh, xh
+    opening = [(Y, 0, 0), (Y, 1, 0), (X, 0, 1), (X, 1, 1)]
+    units_a = opening + [(LOCAL, 0, first), (LOCAL, 1, first), (D1, 0, first), (EXTRA, 0, second),
+                         (D2, 0, second), (EXTRA, 1, second), (D1, 1, first), (D2, 1, second),
+                         (D1F, 0, first), (D1F, 1, first)]
+    units_bz = opening + [(LOCAL, 0, second), (LOCAL, 1, second), (D1F, 0, first), (EXTRA, 0, first),
+                          (D2F, 0, second), (EXTRA, 1, first), (D1F, 1, first), (D1, 0, first),
+                          (D2F, 1, second), (D1, 1, first)]
+    units_bn = opening + [(LOCAL, 0, second), (LOCAL, 1, second), (D1F, 0, first), (D2F, 0, second),
+                          (D1F, 1, first), (D2F, 1, second), (D1, 0, first), (EXTRA, 0, first),
+                          (D1, 1, first), (EXTRA, 1, first)]
+    half = rows // 2
 
     def unit(u, carry):
-        @at(u, is_a, 1)
-        def _():
-            @pl.when(is_z)
-            def _():
-                pl.semaphore_wait(ready, 1)
-                each(send_z)
-
-            relay_a(0)
-
-        @at(u, is_a, 2)
-        def _():
-            relay_a(1)
-
-        @at(u, is_b, 2)
-        def _():
-            relay_b(0)
-
-        @pl.when(u == 2)
-        def _():
-            each(lambda k: arrive(LOCAL, k))
-
-        @at(u, is_a, 3)
-        def _():
-            relay_a(2)
-            both(D2, F_D2)(0)
-            relay_a(3)
-
-            @pl.when(not_z)
-            def _():
-                each(second_a)
-
-            both(D2, F_D2)(1)
-
-            @pl.when(is_z)
-            def _():
-                each(lambda k: arrive(EXTRA, k))
-
-        @at(u, is_b, 3)
-        def _():
-            relay_b(1)
-            relay_b(2)
-            relay_b(3)
-            each(lambda k: arrive(D2F, k))
-
-        @at(u, is_a, 4)
-        def _():
-            @pl.when(is_z)
-            def _():
-                each(second_a)
-
-            both(D2, F_D2)(2)
-            both(D2, F_D2)(3)
-
-        @at(u, is_b, 4)
-        def _():
-            each(lambda k: arrive(D1F, k))
-
-        @pl.when(u == 5)
-        def _():
-            each(both(D1, F_D1))
-
-        @at(u, is_a, 6)
-        def _():
-            each(lambda k: arrive(D1F, k))
-
-        @at(u, is_b, 6)
-        def _():
-            each(lambda k: arrive(EXTRA, k))
-
-        first, second = 1 - xh, xh
-        b = jnp.where(u == 0, Y, jnp.where(u == 1, X, jnp.where(u == 2, LOCAL, jnp.where(u == 3,
-            jnp.where(is_a, EXTRA, D2F), jnp.where(u == 4, jnp.where(is_a, D2, D1F),
-            jnp.where(u == 5, D1, jnp.where(is_a, D1F, EXTRA)))))))
-        in_first = jnp.where(u == 2, is_a, jnp.where(u == 3, False, jnp.where(u == 4, is_b, True)))
-        s = jnp.where(u == 0, 0, jnp.where(u == 1, 1, jnp.where(in_first, first, second)))
-        weigh(s, b, slice(None), u < 2)
+        for cond, number, plan in plans:
+            pl.when(jnp.logical_and(u == number, cond))(plan)
+
+        def pick(field):
+            value = jnp.int32(0)
+            for number, (ua, ubz, ubn) in enumerate(zip(units_a, units_bz, units_bn)):
+                which = jnp.where(is_a, ua[field], jnp.where(is_z, ubz[field], ubn[field]))
+                value = jnp.where(u == number, which, value)
+            return value
+
+        h = pick(1)
+        weigh(pick(2), pick(0), pl.ds(pl.multiple_of(h * half, 16), half), u < 4, h * half)
         return carry
 
-    lax.fori_loop(0, 7, unit, 0)
-
+    lax.fori_loop(0, len(units_a), unit, 0)
     acc[1 - xh] = acc[1 - xh] * factor
 
     @each
@@ -250,7 +373,7 @@
 
         @pl.when(is_b)
         def _():
-            both(D2, F_D2)(k)
+            forward_2(k)
 
         @pl.when(k < CHUNKS - 1)
         def _():

time: 89.4 us -> 84.3 us (0.943)
  Pallas kernels: 87.1 us -> 81.5 us
    pallas_call x1, Pallas kernels: 84.3 us -> 78.7 us  [body(): pl.pallas_call(functools.partial(kernel, lax.axis_size('dp')), out_shape=...]
where the time goes in v4:
time: 84.3 us; the launch traced here: 83.5 us
  Pallas kernels  81.5 us (97%)
  between operations  1.93 us (2%)
    pallas_call x1, Pallas kernels, body(): pl.pallas_call(functools.partial(kernel, lax.axis_size('dp')), out_shape=...  78.7 us
    pallas_call x1, Pallas kernels, body(): pl.pallas_call(finish, out_shape=(out, out), in_specs=[vmem, vmem, smem,...  2.8 us

profile of v4, /device:TPU:1, one launch (start us, length us, event | category | flops | bytes accessed | tf_op | source)
XLA Modules:
  0.0 83.5 jit_solution(4784934090893942212)
XLA Ops:
  1.9 78.7 %pairs.1 = (f32[2,704,1152]{2,1,0:T(8,128)S(1)}, bf16[10,704,1152]{2,1,0:T(8,128)(2,1)S(1)}) custom-call(bf16[704,1152]{1,0:T(8,128)(2,1)} %x_ref.1, bf16[704,1152]{1,0:T(8,128)(2,1)} %y_ref.1, f32[1]{0:T(128)S(6)} %copy.6.scale_ref, f32[1]{0:T(128)S(6)} %copy.7.bias_ref), custom_call_target="tpu_custom_call" | custom-call | flops 18270388224 | bytes 9732096 | tf_op jit(solution)/shard_map/pairs/pallas_call | solution.py:446
  80.7 2.8 %finish.1 = (f32[704,1152]{1,0:T(8,128)}, f32[704,1152]{1,0:T(8,128)}) custom-call(f32[2,704,1152]{2,1,0:T(8,128)S(1)} %get-tuple-element.4.acc, bf16[10,704,1152]{2,1,0:T(8,128)(2,1)S(1)} %get-tuple-element.5.buf, f32[1]{0:T(128)S(6)} %copy.6.scale_ref, f32[1]{0:T(128)S(6)} %copy.7.bias_ref), custom_call_target="tpu_custom_call" | custom-call | tf_op jit(solution)/shard_map/finish/pallas_call | solution.py:465

commit v5 on v4

--- a/solution.py
+++ b/solution.py
@@ -45,8 +45,15 @@
         load.start()
     mesh_id = dict(device_id_type=pl.DeviceIdType.MESH)
     barrier = pltpu.get_barrier_semaphore()
-    for peer in (cut, side, sibling):
-        pl.semaphore_signal(barrier, inc=1, device_id=peer, **mesh_id)
+    a_z, b_z = jnp.logical_and(is_a, is_z), jnp.logical_and(is_b, is_z)
+    b_n = jnp.logical_and(is_b, not_z)
+
+    pl.semaphore_signal(barrier, inc=1, device_id=(cut[0], jnp.where(is_z, 3 - 3 * xh, cut[1])), **mesh_id)
+    pl.semaphore_signal(barrier, inc=1, device_id=(side[0], jnp.where(is_z, side[1], 3 * xh)), **mesh_id)
+
+    @pl.when(jnp.logical_not(a_z))
+    def _():
+        pl.semaphore_signal(barrier, inc=1, device_id=sibling, **mesh_id)
 
     @pl.when(is_z)
     def _():
@@ -57,11 +64,17 @@
     for load in loads:
         load.wait()
 
-    pl.semaphore_wait(barrier, 3 + 4 * z * (1 - a))
-
-    @pl.when(jnp.logical_and(is_z, is_b))
+    @pl.when(jnp.logical_not(b_z))
+    def _():
+        pl.semaphore_wait(barrier, 3 + 2 * z)
+
+    @pl.when(a_z)
     def _():
         pl.semaphore_signal(ready, inc=1, device_id=sibling, **mesh_id)
+
+    @pl.when(b_z)
+    def _():
+        pl.semaphore_wait(ready, 1)
 
     def span(k):
         return pl.ds(pl.multiple_of(k * part, 16), part)
@@ -100,15 +113,17 @@
         def _():
             copy(F_P1, first_src, jnp.where(is_z, EXTRA, TRANSIT), side, k).start()
 
-        @pl.when(jnp.logical_and(is_z, is_b))
-        def _():
-            send_z(k)
-
         @pl.when(jnp.logical_and(not_z, is_b))
         def _():
             copy(F_P2, second_from, D2, cut, k).start()
 
         copy(F_LOCAL, 1 - core, LOCAL, sibling, k).start()
+
+    @pl.when(b_z)
+    def _():
+        pl.semaphore_wait(barrier, 4)
+        pl.semaphore_signal(ready, inc=1, device_id=sibling, **mesh_id)
+        each(send_z)
 
     def relay_a(k):
         held = jnp.where(is_z, TRANSIT, EXTRA)
@@ -165,9 +180,6 @@
         return lambda body: plans.append((cond, number, body))
 
     plans = []
-
-    a_z, b_z = jnp.logical_and(is_a, is_z), jnp.logical_and(is_b, is_z)
-    b_n = jnp.logical_and(is_b, not_z)
 
     @before(a_z, 2)
     def _():

time: 84.3 us -> 83.6 us (level)
  no operation moved by 1% of the time
where the time goes in v5:
time: 83.6 us; the launch traced here: 83.5 us
  Pallas kernels  81.6 us (98%)
  between operations  1.93 us (2%)
    pallas_call x1, Pallas kernels, body(): pl.pallas_call(functools.partial(kernel, lax.axis_size('dp')), out_shape=...  78.8 us
    pallas_call x1, Pallas kernels, body(): pl.pallas_call(finish, out_shape=(out, out), in_specs=[vmem, vmem, smem,...  2.8 us

profile of v5, /device:TPU:1, one launch (start us, length us, event | category | flops | bytes accessed | tf_op | source)
XLA Modules:
  0.0 83.5 jit_solution(10935553475097753474)
XLA Ops:
  1.9 78.8 %pairs.1 = (f32[2,704,1152]{2,1,0:T(8,128)S(1)}, bf16[10,704,1152]{2,1,0:T(8,128)(2,1)S(1)}) custom-call(bf16[704,1152]{1,0:T(8,128)(2,1)} %x_ref.1, bf16[704,1152]{1,0:T(8,128)(2,1)} %y_ref.1, f32[1]{0:T(128)S(6)} %copy.6.scale_ref, f32[1]{0:T(128)S(6)} %copy.7.bias_ref), custom_call_target="tpu_custom_call" | custom-call | flops 18270388224 | bytes 9732096 | tf_op jit(solution)/shard_map/pairs/pallas_call | solution.py:458
  80.7 2.8 %finish.1 = (f32[704,1152]{1,0:T(8,128)}, f32[704,1152]{1,0:T(8,128)}) custom-call(f32[2,704,1152]{2,1,0:T(8,128)S(1)} %get-tuple-element.4.acc, bf16[10,704,1152]{2,1,0:T(8,128)(2,1)S(1)} %get-tuple-element.5.buf, f32[1]{0:T(128)S(6)} %copy.6.scale_ref, f32[1]{0:T(128)S(6)} %copy.7.bias_ref), custom_call_target="tpu_custom_call" | custom-call | tf_op jit(solution)/shard_map/finish/pallas_call | solution.py:477

commit v6 on v5

--- a/solution.py
+++ b/solution.py
@@ -61,8 +61,6 @@
             pl.semaphore_signal(barrier, inc=1, device_id=(along_z(sign)[0], xh * 2 + 1 - xh), **mesh_id)
 
     acc[...] = jnp.zeros_like(acc)
-    for load in loads:
-        load.wait()
 
     @pl.when(jnp.logical_not(b_z))
     def _():
@@ -103,16 +101,30 @@
     def send_z(k):
         copy(F_Z, second_src, ZIN, along_z(z_second), k).start()
 
+    def send_first(ref, k):
+        def go(dst, peer):
+            pltpu.make_async_remote_copy(
+                src_ref=ref.at[span(k)],
+                dst_ref=buf.at[dst, span(k)],
+                send_sem=send_sem.at[F_P1, k],
+                recv_sem=recv_sem.at[dst, k],
+                device_id=peer,
+                **mesh_id,
+            ).start()
+
+        pl.when(is_a)(lambda: go(TRANSIT, cut))
+        pl.when(is_b)(lambda: go(jnp.where(is_z, EXTRA, TRANSIT), side))
+
     @each
     def _(k):
-        @pl.when(is_a)
-        def _():
-            copy(F_P1, first_src, TRANSIT, cut, k).start()
-
-        @pl.when(is_b)
-        def _():
-            copy(F_P1, first_src, jnp.where(is_z, EXTRA, TRANSIT), side, k).start()
-
+        pl.when(xh == 0)(lambda: send_first(y_ref, k))
+        pl.when(xh == 1)(lambda: send_first(x_ref, k))
+
+    for load in loads:
+        load.wait()
+
+    @each
+    def _(k):
         @pl.when(jnp.logical_and(not_z, is_b))
         def _():
             copy(F_P2, second_from, D2, cut, k).start()

time: 83.6 us -> 83.8 us (level)
  no operation moved by 1% of the time
where the time goes in v6:
time: 83.8 us; the launch traced here: 83.7 us
  Pallas kernels  81.8 us (98%)
  between operations  1.93 us (2%)
    pallas_call x1, Pallas kernels, body(): pl.pallas_call(functools.partial(kernel, lax.axis_size('dp')), out_shape=...  79 us
    pallas_call x1, Pallas kernels, body(): pl.pallas_call(finish, out_shape=(out, out), in_specs=[vmem, vmem, smem,...  2.8 us

profile of v6, /device:TPU:1, one launch (start us, length us, event | category | flops | bytes accessed | tf_op | source)
XLA Modules:
  0.0 83.7 jit_solution(210054565506060620)
XLA Ops:
  1.9 79.0 %pairs.1 = (f32[2,704,1152]{2,1,0:T(8,128)S(1)}, bf16[10,704,1152]{2,1,0:T(8,128)(2,1)S(1)}) custom-call(bf16[704,1152]{1,0:T(8,128)(2,1)} %x_ref.1, bf16[704,1152]{1,0:T(8,128)(2,1)} %y_ref.1, f32[1]{0:T(128)S(6)} %copy.6.scale_ref, f32[1]{0:T(128)S(6)} %copy.7.bias_ref), custom_call_target="tpu_custom_call" | custom-call | flops 18270388224 | bytes 9732096 | tf_op jit(solution)/shard_map/pairs/pallas_call | solution.py:470
  80.9 2.8 %finish.1 = (f32[704,1152]{1,0:T(8,128)}, f32[704,1152]{1,0:T(8,128)}) custom-call(f32[2,704,1152]{2,1,0:T(8,128)S(1)} %get-tuple-element.4.acc, bf16[10,704,1152]{2,1,0:T(8,128)(2,1)S(1)} %get-tuple-element.5.buf, f32[1]{0:T(128)S(6)} %copy.6.scale_ref, f32[1]{0:T(128)S(6)} %copy.7.bias_ref), custom_call_target="tpu_custom_call" | custom-call | tf_op jit(solution)/shard_map/finish/pallas_call | solution.py:489
